TPU v7x, 32 devices: a whole 2x2x4 slice. The times are simulated.
32 devices in a mesh: sub: 4 (over z), cgrp: 8 (over y, x, core).
Axes of the slice: x: 2, y: 2, z: 4, core: 2. Of those that a mesh axis runs over, the one named last changes fastest.
Arguments:
- source: float32 [256, 32768], P('sub', 'cgrp'), may hold values from -7.5 to 7.5
- capacity: float32 [256, 32768], P('sub', 'cgrp'), may hold values from 0.01 to 1
- fd_weights: float32 [256, 32768], P('sub', 'cgrp'), may hold values from 0.02 to 1
- fd_modes: float32 [3, 64, 64], replicated, may hold values from -0.75 to 0.75
- face_modes: float32 [2, 128, 64], replicated, may hold values from -0.75 to 0.75
- coarse_map: int32 [4, 8, 6, 128], P('sub', 'cgrp'), may hold values from 0 to 24575, as said below
- fsai_cols: int32 [192, 8], P(('sub', 'cgrp')), may hold values from 0 to 191
- fsai_blocks: float32 [192, 8, 128, 128], P(('sub', 'cgrp')), may hold values from -0.1875 to 0.1875
Outputs:
- solution: float32 [256, 32768], P('sub', 'cgrp')
- residual: float32 [256, 32768], P('sub', 'cgrp')
Inputs may be any that keep to these rules, and one draw needn't show every extreme that they name: `coarse_map`: entries are numbered by owner: with d = s * 8 + t, face f of subdomain (s, t) takes the entries (6 d + f) * 128 to (6 d + f) * 128 + 127, each once, in an order of its own; except that face 0 of a subdomain with s > 0 takes exactly the entries of face 1 of subdomain (s - 1, t), and face 2 of a subdomain with t > 0 exactly those of face 3 of subdomain (s, t - 1), function k of both sides taking the same entry.
All inputs are finite; a program needn't handle non-finite values.
Results may differ from a plain program's by a relative error of at most 0.0001.
Values sent between devices are 32-bit elements; how exact they have to be, the bound alone decides.
A program may use at most 64 MiB of HBM per device.

v0:
```python
import jax
import jax.numpy as jnp
from jax import lax
from jax.sharding import PartitionSpec as P

C = 64
highest = lax.Precision.HIGHEST
along_first = 1.0
along_second = 0.6
along_third = 2.5


def with_halo(array, sides, width):
    for axis, dim in sides:
        count, length = (lax.axis_size(axis), array.shape[dim])
        up = [(i, (i + 1) % count) for i in range(count - 1)]
        down = [(j, i) for i, j in up]
        last = lax.slice_in_dim(array, length - width, length, axis=dim)
        first = lax.slice_in_dim(array, 0, width, axis=dim)
        before = lax.ppermute(last, axis, up)
        after = lax.ppermute(first, axis, down)
        array = jnp.concatenate([before, array, after], axis=dim)
    return array


def operate(field, capacity):
    padded = with_halo(field, (("sub", 0), ("cgrp", 1)), 1)
    padded = jnp.pad(padded, ((0, 0), (0, 0), (1, 1)))
    first = padded[2:, 1:-1, 1:-1] + padded[:-2, 1:-1, 1:-1]
    second = padded[1:-1, 2:, 1:-1] + padded[1:-1, :-2, 1:-1]
    third = padded[1:-1, 1:-1, 2:] + padded[1:-1, 1:-1, :-2]
    diagonal = capacity + 2.0 * (along_first + along_second + along_third)
    return diagonal * field - along_first * first - along_second * second - along_third * third


def transform(blocks, modes):
    blocks = jnp.einsum("ai,...ijk->...ajk", modes[0], blocks, precision=highest)
    blocks = jnp.einsum("bj,...ajk->...abk", modes[1], blocks, precision=highest)
    return jnp.einsum("ck,...abk->...abc", modes[2], blocks, precision=highest)


def transform_back(blocks, modes):
    blocks = jnp.einsum("ai,...ajk->...ijk", modes[0], blocks, precision=highest)
    blocks = jnp.einsum("bj,...ibk->...ijk", modes[1], blocks, precision=highest)
    return jnp.einsum("ck,...ijc->...ijk", modes[2], blocks, precision=highest)


def face_planes(blocks):
    return jnp.stack(
        [
            blocks[..., 0, :, :],
            blocks[..., -1, :, :],
            blocks[..., :, 0, :],
            blocks[..., :, -1, :],
            blocks[..., :, :, 0],
            blocks[..., :, :, -1],
        ],
        axis=-3,
    )


def restrict(planes, face_modes):
    partial_rows = jnp.einsum("ka,...fab->...fkb", face_modes[0], planes, precision=highest)
    return jnp.sum(partial_rows * face_modes[1], axis=-1)


def extend(values, face_modes):
    return jnp.einsum(
        "ka,...fkb->...fab", face_modes[0], values[..., None] * face_modes[1], precision=highest
    )


def add_planes(blocks, planes):
    blocks = blocks.at[..., 0, :, :].add(planes[..., 0, :, :])
    blocks = blocks.at[..., -1, :, :].add(planes[..., 1, :, :])
    blocks = blocks.at[..., :, 0, :].add(planes[..., 2, :, :])
    blocks = blocks.at[..., :, -1, :].add(planes[..., 3, :, :])
    blocks = blocks.at[..., :, :, 0].add(planes[..., 4, :, :])
    blocks = blocks.at[..., :, :, -1].add(planes[..., 5, :, :])
    return blocks


def coarse_apply(coarse, fsai_cols, fsai_blocks):
    table = coarse.reshape(-1, fsai_blocks.shape[2])
    picked = table[fsai_cols]
    image = jnp.einsum("rnij,rnj->ri", fsai_blocks, picked, precision=highest)
    spread = jnp.einsum("rnij,ri->rnj", fsai_blocks, image, precision=highest)
    return jnp.zeros_like(table).at[fsai_cols].add(spread).reshape(-1)


def coarse_round(coarse_local, coarse_map, fsai_cols, fsai_blocks):
    slots = coarse_map.reshape(-1)
    length = fsai_blocks.shape[0] * fsai_blocks.shape[2] * lax.axis_size(("sub", "cgrp"))
    term = jnp.zeros((length,), jnp.float32).at[slots].add(coarse_local.reshape(-1))
    coarse = lax.psum(term, ("sub", "cgrp"))
    back = lax.psum(coarse_apply(coarse, fsai_cols, fsai_blocks), ("sub", "cgrp"))
    return back[slots].reshape(coarse_local.shape)


def precondition(residual, fd_weights, fd_modes, face_modes, coarse_map, fsai_cols, fsai_blocks):
    local = transform_back(fd_weights * transform(residual, fd_modes), fd_modes)
    coarse_local = restrict(face_planes(residual), face_modes)
    correction = coarse_round(coarse_local, coarse_map, fsai_cols, fsai_blocks)
    return add_planes(local, extend(correction, face_modes))


def inner_sum(left, right):
    return lax.psum(jnp.sum(left * right), ("sub", "cgrp"))


def curvature_sum(left, right):
    return lax.psum(jnp.sum(left * right), ("sub", "cgrp"))


def body(source, capacity, fd_weights, fd_modes, face_modes, coarse_map, fsai_cols, fsai_blocks):
    cube = (C, C, C)
    flat_shape = source.shape
    source = source.reshape(cube)
    capacity = capacity.reshape(cube)
    fd_weights = fd_weights.reshape(cube)
    residual = source
    precond = precondition(
        residual, fd_weights, fd_modes, face_modes, coarse_map, fsai_cols, fsai_blocks
    )
    gamma = inner_sum(residual, precond)
    image = operate(precond, capacity)
    alpha = gamma / curvature_sum(precond, image)
    solution = alpha * precond
    residual = residual - alpha * image
    return (solution.reshape(flat_shape), residual.reshape(flat_shape))


def solution(mesh):
    in_specs = (
        P("sub", "cgrp"),
        P("sub", "cgrp"),
        P("sub", "cgrp"),
        P(),
        P(),
        P("sub", "cgrp", None, None),
        P(("sub", "cgrp"), None),
        P(("sub", "cgrp"), None, None, None),
    )
    out_specs = (P("sub", "cgrp"), P("sub", "cgrp"))
    return jax.shard_map(body, mesh=mesh, in_specs=in_specs, out_specs=out_specs, check_vma=False)
```

profile of v0, /device:TPU:0, one launch (start us, length us, event | category | flops | bytes accessed | tf_op | source)
XLA Modules:
  0.0 433.0 jit_solution(17539706606090331872)
XLA Ops:
  7.2 1.2 slice_reduce_fusion
  8.4 3.1 reshape.238
  11.5 1.7 fusion.60
  13.2 5.0 %fusion.59 = (f32[64,64,1]{2,1,0:T(8,128)}, f32[64,64,1]{2,1,0:T(8,128)}) fusion(f32[64,64,64]{2,1,0:T(8,128)} %reshape.238), kind=kLoop, calls=%fused_computation.103 | loop fusion | bytes 65536 | tf_op jit(solution)/shard_map/slice | solution.py:56
  18.3 0.7 copy.89
  19.2 1.5 copy.122
  20.6 0.7 copy.121
  21.4 3.3 copy.124
  24.6 3.2 copy.123
  27.8 0.8 constant_dynamic-update-slice_fusion
  28.6 0.8 bitcast_dynamic-update-slice_fusion.3
  29.4 0.8 bitcast_dynamic-update-slice_fusion.2
  30.1 0.8 bitcast_dynamic-update-slice_fusion.1
  30.9 0.8 bitcast_dynamic-update-slice_fusion
  31.6 0.3 fusion.25
  32.0 6.5 %scatter_custom_fusion = f32[24576]{0:T(1024)} fusion(s32[768]{0:T(1024)S(1)} %fusion.53, f32[768]{0:T(1024)S(1)} %bitcast.105, f32[]{:T(128)} %constant.167.clone.1), kind=kCustom, calls=%fused_computation.52 | custom fusion | flops 768 | bytes 98308 | tf_op jit(solution)/shard_map/scatter-add | solution.py:94
  38.5 0.6 all-reduce.7.cloned.1.call-start
  39.2 4.6 %fusion.16 = f32[64,64,64]{2,0,1:T(8,128)S(1)} fusion(f32[64,64,64]{2,1,0:T(8,128)} %reshape.238, f32[3,64,64]{2,1,0:T(8,128)S(1)} %copy-done.7), kind=kOutput, calls=%fused_computation.36 | convolution fusion | flops 201326592 | bytes 2129920 | tf_op jit(solution)/shard_map/ai,...ijk->...ajk/dot_general | solution.py:37
  43.7 5.6 %fusion.14 = f32[64,64,64]{2,1,0:T(8,128)} fusion(f32[64,64,64]{2,0,1:T(8,128)S(1)} %fusion.16, f32[3,64,64]{2,1,0:T(8,128)S(1)} %copy-done.7), kind=kOutput, calls=%fused_computation.34 | convolution fusion | flops 201326592 | bytes 3178496 | tf_op jit(solution)/shard_map/bj,...ajk->...abk/dot_general | solution.py:38
  49.3 3.3 reshape.239
  52.6 5.8 %fusion.21 = f32[64,64,64]{2,1,0:T(8,128)S(1)} fusion(f32[64,64,64]{2,1,0:T(8,128)} %reshape.239, f32[64,64,64]{2,1,0:T(8,128)} %fusion.14, f32[3,64,64]{2,1,0:T(8,128)S(1)} %copy-done.7), kind=kOutput, calls=%fused_computation.42 | convolution fusion | flops 201588736 | bytes 3178496 | tf_op jit(solution)/shard_map/ck,...abk->...abc/dot_general | solution.py:39
  58.4 5.6 %fusion.18 = f32[64,64,64]{0,2,1:T(8,128)} fusion(f32[64,64,64]{2,1,0:T(8,128)S(1)} %fusion.21, f32[3,64,64]{2,1,0:T(8,128)S(1)} %copy-done.7), kind=kOutput, calls=%fused_computation.41 | convolution fusion | flops 201326592 | bytes 3178496 | tf_op jit(solution)/shard_map/ai,...ajk->...ijk/dot_general | solution.py:43
  64.0 4.3 %copy.80 = f32[64,64,64]{1,2,0:T(8,128)} copy(f32[64,64,64]{0,2,1:T(8,128)} %fusion.18) | data formatting | bytes 2097152 | tf_op jit(solution)/shard_map/ai,...ajk->...ijk/dot_general | solution.py:43
  68.4 3.5 fusion.40
  71.8 3.4 fusion.8
  75.2 86.7 %all-reduce.5.cloned.1.call-done = f32[192,128]{1,0:T(8,128)} async-done(((f32[192,128]{1,0:T(8,128)}), f32[192,128]{1,0:T(8,128)}) %all-reduce.5.cloned.1.call-update) | async-done | bytes 98320 | tf_op jit(solution)/shard_map/psum | solution.py:95
  161.9 1.5 gather_fusion
  163.4 2.7 fusion.62
  166.1 1.6 fusion.54
  167.7 1.4 scatter_custom_fusion.1
  169.2 121.4 %all-reduce.7.cloned.1.call-done = f32[24576]{0:T(1024)} async-done(((f32[24576]{0:T(1024)}), f32[24576]{0:T(1024)}) %all-reduce.7.cloned.1.call-update) | async-done | bytes 98320 | tf_op jit(solution)/shard_map/psum | solution.py:96
  290.6 5.0 %gather_fusion.1 = f32[768]{0:T(1024)S(1)} fusion(f32[24576]{0:T(1024)} %all-reduce.7.cloned.1.call-done, s32[1024]{0:T(1024)S(1)} %pad_clamp_fusion), kind=kCustom, calls=%fused_computation.1 | custom fusion | bytes 9216 | tf_op jit(solution)/shard_map/gather | solution.py:97
  295.6 0.7 convolution_bitcast_fusion
  296.6 0.7 copy.126
  297.3 2.1 copy.95
  299.4 5.1 %scatter-add.48 = f32[64,64,64]{1,2,0:T(8,128)S(1)} dynamic-update-slice(f32[64,64,64]{1,2,0:T(8,128)S(1)} %constant_dynamic-update-slice_fusion.2, f32[64,1,64]{1,2,0:T(8,128)} %copy.95, s32[]{:T(128)} %constant.168.clone.1, s32[]{:T(128)} %constant.168.clone.1, s32[]{:T(128)} %constant.168.clone.1) | dynamic-update-slice | bytes 32772 | tf_op jit(solution)/shard_map/scatter-add | solution.py:76
  304.4 2.0 slice.283
  306.4 2.3 copy.127
  308.7 2.1 copy.97
  310.7 8.4 %scatter-add.49 = f32[64,64,64]{1,2,0:T(8,128)S(1)} dynamic-update-slice(f32[64,64,64]{1,2,0:T(8,128)S(1)} %scatter-add.48, f32[64,1,64]{1,2,0:T(8,128)} %copy.97, s32[]{:T(128)} %constant.168.clone.1, s32[]{:T(128)} %constant.171.clone.1, s32[]{:T(128)} %constant.168.clone.1) | dynamic-update-slice | bytes 32772 | tf_op jit(solution)/shard_map/scatter-add | solution.py:77
  319.6 5.1 %collective-permute-start.1 = (f32[1,64,64]{1,2,0:T(8,128)S(1)}, f32[1,64,64]{1,2,0:T(8,128)S(1)}, u32[]{:S(2)}, u32[]{:S(2)}) collective-permute-start(f32[1,64,64]{1,2,0:T(8,128)S(1)} %get-tuple-element.83), channel_id=1, source_target_pairs={{0,8},{8,16},{16,24},{1,9},{9,17},{17,25},{2,10},{10,18},{18,26},{... | collective-permute-start | bytes 49160 | tf_op jit(solution)/shard_map/ppermute | solution.py:20
  324.8 1.3 collective-permute-start
  326.3 4.2 collective-permute-done
  330.8 2.8 fusion.57
  333.5 2.8 copy.104
  336.3 2.8 copy.102
  339.1 1.3 collective-permute-start.2
  340.4 3.0 collective-permute-start.3
  343.4 1.3 broadcast_add_fusion
  344.7 3.1 copy.100
  347.8 2.2 add.99
  350.0 2.9 copy.101
  353.0 3.0 copy.105
  356.0 3.1 copy.103
  359.1 3.7 select_maximum_fusion
  362.8 0.4 copy-done.5
  363.3 0.6 copy-done.6
  363.9 6.5 %multiply_reduce_fusion = (f32[]{:T(128)}, f32[]{:T(128)}, f32[64,64,64]{1,2,0:T(8,128)}) fusion(f32[64,64,64]{1,2,0:T(8,128)S(1)} %scatter-add.51, f32[64,64,64]{1,2,0:T(8,128)S(1)} %copy-done.5, f32[66,66,66]{1,2,0:T(8,128)S(1)} %select_maximum_fusion, f32[1,64,64]{1,2,0:T(8,128)S(1)} %collective-permute-done, f32[1,64,64]{1,2,0:T(8,128)S(1)} %collective-permute-done.1, ...), kind=kLoop, calls=%fused_computation.39 | loop fusion | flops 5505022 | bytes 6358024 | tf_op jit(solution)/shard_map/reduce_sum | solution.py:112
  370.4 39.3 %all-reduce.1 = (f32[]{:T(128)}, f32[]{:T(128)}) all-reduce(f32[]{:T(128)} %get-tuple-element.75, f32[]{:T(128)} %get-tuple-element.74), channel_id=1, replica_groups=mesh['sub'=4,'cgrp'=8] {'sub','cgrp'}, use_global_device_ids=true, to_apply=%region_6.0 | all-reduce | flops 2 | bytes 16 | tf_op jit(solution)/shard_map/psum | solution.py:108
  411.1 5.4 %multiply_subtract_fusion = (f32[64,64,64]{1,2,0:T(8,128)}, f32[64,64,64]{1,2,0:T(8,128)}) fusion(f32[64,64,64]{1,2,0:T(8,128)} %copy.100, f32[64,64,64]{1,2,0:T(8,128)} %get-tuple-element.80, f32[]{:T(128)S(6)} %div.3, f32[64,64,64]{1,2,0:T(8,128)S(1)} %scatter-add.51), kind=kLoop, calls=%fused_computation.38 | loop fusion | flops 786432 | bytes 5242884 | tf_op jit(solution)/shard_map/sub | solution.py:129
  416.4 1.9 copy.110
  418.4 1.6 reshape.249
  420.0 3.1 copy.108
  423.1 2.9 reshape.248
  (57 shorter events, 1.7 us)
Async XLA Ops:
  7.2 156.2 %copy-start = (f32[6,8,128,128]{3,2,1,0:T(8,128)S(1)}, f32[6,8,128,128]{3,2,1,0:T(8,128)}, u32[]{:S(2)}) copy-start(f32[6,8,128,128]{3,2,1,0:T(8,128)} %param.27) | copy-start | bytes 9437188
  7.2 154.7 %all-reduce.5.cloned.1.call-start = ((), (), s32[]{:S(2)}) async-start(), calls=%async_computation | async-start | bytes 196608 | tf_op jit(solution)/shard_map/psum | solution.py:95
  13.2 5.0 %copy-start.10 = (s32[1,1,6,128]{3,1,2,0:T(1,128)S(1)}, s32[1,1,6,128]{3,1,2,0:T(1,128)}, u32[]{:S(2)}) copy-start(s32[1,1,6,128]{3,1,2,0:T(1,128)} %param.25) | copy-start | bytes 9220
  13.2 5.0 %copy-start.8 = (f32[2,128,64]{1,2,0:T(8,128)S(1)}, f32[2,128,64]{1,2,0:T(8,128)}, u32[]{:S(2)}) copy-start(f32[2,128,64]{1,2,0:T(8,128)} %param.24) | copy-start | bytes 196612
  21.3 17.7 %copy-start.9 = (s32[6,8]{1,0:T(8,128)S(1)}, s32[6,8]{1,0:T(8,128)}, u32[]{:S(2)}) copy-start(s32[6,8]{1,0:T(8,128)} %param.26) | copy-start | bytes 580
  21.3 17.8 %copy-start.7 = (f32[3,64,64]{2,1,0:T(8,128)S(1)}, f32[3,64,64]{2,1,0:T(8,128)}, u32[]{:S(2)}) copy-start(f32[3,64,64]{2,1,0:T(8,128)} %param.23) | copy-start | bytes 147460
  38.5 252.1 %all-reduce.7.cloned.1.call-start = ((), (), s32[]{:S(2)}) async-start(), calls=%async_computation.1 | async-start | bytes 196608 | tf_op jit(solution)/shard_map/psum | solution.py:96
  166.1 3.0 slice-start
  169.1 127.3 %copy-start.2 = (f32[64,64,64]{1,2,0:T(8,128)S(1)}, f32[64,64,64]{1,2,0:T(8,128)}, u32[]{:S(2)}) copy-start(f32[64,64,64]{1,2,0:T(8,128)} %fusion.8) | copy-start | bytes 3145732
  319.6 6.7 %collective-permute-start.1 = (f32[1,64,64]{1,2,0:T(8,128)S(1)}, f32[1,64,64]{1,2,0:T(8,128)S(1)}, u32[]{:S(2)}, u32[]{:S(2)}) collective-permute-start(f32[1,64,64]{1,2,0:T(8,128)S(1)} %get-tuple-element.83), channel_id=1, source_target_pairs={{0,8},{8,16},{16,24},{1,9},{9,17},{17,25},{2,10},{10,18},{18,26},{... | collective-permute-start | bytes 49160 | tf_op jit(solution)/shard_map/ppermute | solution.py:20
  324.8 5.8 %collective-permute-start = (f32[1,64,64]{1,2,0:T(8,128)S(1)}, f32[1,64,64]{1,2,0:T(8,128)S(1)}, u32[]{:S(2)}, u32[]{:S(2)}) collective-permute-start(f32[1,64,64]{1,2,0:T(8,128)S(1)} %get-tuple-element.84), channel_id=1, source_target_pairs={{8,0},{16,8},{24,16},{9,1},{17,9},{25,17},{10,2},{18,10},{26,18},{... | collective-permute-start | bytes 49160 | tf_op jit(solution)/shard_map/ppermute | solution.py:21
  339.1 16.9 %collective-permute-start.2 = (f32[66,1,64]{0,2,1:T(8,128)S(1)}, f32[66,1,64]{0,2,1:T(8,128)S(1)}, u32[]{:S(2)}, u32[]{:S(2)}) collective-permute-start(f32[66,1,64]{0,2,1:T(8,128)S(1)} %copy.102), channel_id=1, source_target_pairs={{1,0},{2,1},{3,2},{4,3},{5,4},{6,5},{7,6},{9,8},{10,9},{11,10},{12... | collective-permute-start | bytes 50696 | tf_op jit(solution)/shard_map/ppermute | solution.py:21
  340.4 12.6 %collective-permute-start.3 = (f32[66,1,64]{0,2,1:T(8,128)S(1)}, f32[66,1,64]{0,2,1:T(8,128)S(1)}, u32[]{:S(2)}, u32[]{:S(2)}) collective-permute-start(f32[66,1,64]{0,2,1:T(8,128)S(1)} %copy.104), channel_id=1, source_target_pairs={{0,1},{1,2},{2,3},{3,4},{4,5},{5,6},{6,7},{8,9},{9,10},{10,11},{11... | collective-permute-start | bytes 50696 | tf_op jit(solution)/shard_map/ppermute | solution.py:20
  359.1 3.8 copy-start.3
  359.1 3.8 copy-start.4
  359.1 4.2 copy-start.5
  359.1 4.8 %copy-start.6 = (f32[64,64,64]{1,2,0:T(8,128)S(1)}, f32[64,64,64]{1,2,0:T(8,128)}, u32[]{:S(2)}) copy-start(f32[64,64,64]{1,2,0:T(8,128)} %copy.101) | copy-start | bytes 3145732
  420.0 6.0 %copy-start.1 = (f32[6,8,128,128]{3,2,1,0:T(8,128)S(1)}, f32[6,8,128,128]{3,2,1,0:T(8,128)}, u32[]{:S(2)}) copy-start(f32[6,8,128,128]{3,2,1,0:T(8,128)} %param.27) | copy-start | bytes 9437188
Sparse Core Ops, SparseCore 0:
  38.6 123.2 all-reduce.4
  169.2 121.3 all-reduce.6
where the time goes:
time: 439 us; the launch traced here: 433 us
  waiting for transfers between devices  213 us (49%)
  local copies, waits for them, and re-layouts  94.9 us (22%)
  blocking collectives  39.3 us (9%)
  matrix products  33.6 us (8%)
  other arithmetic  25.1 us (6%)
  between operations  15.9 us (4%)
  starting transfers between devices  11.4 us (3%)
    psum x1, waiting for transfers between devices, coarse_round(): lax.psum(coarse_apply(coarse, fsai_cols, fsai_blocks), ('sub', 'cgrp'))  121 us
    psum x1, waiting for transfers between devices, coarse_round(): coarse = lax.psum(term, ('sub', 'cgrp'))  86.7 us
    psum x1, blocking collectives, inner_sum(): return lax.psum(jnp.sum(left * right), ('sub', 'cgrp'))  39.3 us
    unnamed x35, local copies, waits for them, and re-layouts  15.9 us
  transfers between devices with their start and end apart: 6, of which 4 were waited for; matrix products, arithmetic and copies ran while one was open for 11% of the time, Pallas kernels for 0%

commit v1 on v0

--- a/solution.py
+++ b/solution.py
@@ -93,7 +93,7 @@
     length = fsai_blocks.shape[0] * fsai_blocks.shape[2] * lax.axis_size(("sub", "cgrp"))
     term = jnp.zeros((length,), jnp.float32).at[slots].add(coarse_local.reshape(-1))
     coarse = lax.psum(term, ("sub", "cgrp"))
-    back = lax.psum(coarse_apply(coarse, fsai_cols, fsai_blocks), ("sub", "cgrp"))
+    back = lax.psum(lax.psum(coarse_apply(coarse, fsai_cols, fsai_blocks), "cgrp"), "sub")
     return back[slots].reshape(coarse_local.shape)
 
 

time: 439 us -> 406 us (0.925)
  waiting for transfers between devices: 213 us -> 180 us
    psum x1 -> x2, waiting for transfers between devices: 121 us -> 86.3 us  [the longest x1 48.9 us: coarse_round(): lax.psum(coarse_apply(coarse, fsai_cols, fsai_blocks), 'cgrp')]
    unnamed x35 -> x33, local copies, waits for them, and re-layouts: 15.9 us -> 15.9 us
  transfers between devices with their start and end apart: 6 -> 7, of which waited for: 4 -> 5; matrix products, arithmetic and copies ran while one was open for 11% -> 13% of each run, Pallas kernels for 0% -> 0%
where the time goes in v1:
time: 406 us; the launch traced here: 400 us
  waiting for transfers between devices  180 us (44%)
  local copies, waits for them, and re-layouts  94.9 us (23%)
  blocking collectives  40.2 us (10%)
  matrix products  35.1 us (9%)
  other arithmetic  25.1 us (6%)
  between operations  15.6 us (4%)
  starting transfers between devices  9.53 us (2%)
    psum x1, waiting for transfers between devices, coarse_round(): coarse = lax.psum(term, ('sub', 'cgrp'))  88.8 us
    psum x1, waiting for transfers between devices, coarse_round(): lax.psum(coarse_apply(coarse, fsai_cols, fsai_blocks), 'cgrp')  48.9 us
    psum x1, blocking collectives, inner_sum(): return lax.psum(jnp.sum(left * right), ('sub', 'cgrp'))  40.2 us
    psum x1, waiting for transfers between devices, coarse_round(): lax.psum(lax.psum(coarse_apply(coarse, fsai_cols, fsai_blocks), 'cgrp'),...  37.5 us
    unnamed x33, local copies, waits for them, and re-layouts  15.9 us
    scatter-add x1, local copies, waits for them, and re-layouts, add_planes(): blocks = blocks.at[..., :, -1, :].add(planes[..., 3, :, :])  8.36 us
  transfers between devices with their start and end apart: 7, of which 5 were waited for; matrix products, arithmetic and copies ran while one was open for 13% of the time, Pallas kernels for 0%

profile of v1, /device:TPU:0, one launch (start us, length us, event | category | flops | bytes accessed | tf_op | source)
XLA Modules:
  0.0 400.1 jit_solution(4953499786821430908)
XLA Ops:
  7.2 1.2 slice_reduce_fusion
  8.4 3.1 reshape.238
  11.5 1.7 fusion.60
  13.2 5.0 %fusion.59 = (f32[64,64,1]{2,1,0:T(8,128)}, f32[64,64,1]{2,1,0:T(8,128)}) fusion(f32[64,64,64]{2,1,0:T(8,128)} %reshape.238), kind=kLoop, calls=%fused_computation.103 | loop fusion | bytes 65536 | tf_op jit(solution)/shard_map/slice | solution.py:56
  18.3 0.7 copy.89
  19.2 1.5 copy.122
  20.6 0.7 copy.121
  21.4 3.3 copy.124
  24.6 3.2 copy.123
  27.8 0.8 constant_dynamic-update-slice_fusion
  28.6 0.8 bitcast_dynamic-update-slice_fusion.3
  29.4 0.8 bitcast_dynamic-update-slice_fusion.2
  30.1 0.8 bitcast_dynamic-update-slice_fusion.1
  30.9 0.8 bitcast_dynamic-update-slice_fusion
  32.0 6.5 %scatter_custom_fusion = f32[24576]{0:T(1024)} fusion(s32[768]{0:T(1024)S(1)} %fusion.53, f32[768]{0:T(1024)S(1)} %bitcast.105, f32[]{:T(128)} %constant.167.clone.1), kind=kCustom, calls=%fused_computation.52 | custom fusion | flops 768 | bytes 98308 | tf_op jit(solution)/shard_map/scatter-add | solution.py:94
  38.5 0.6 all-reduce.8.cloned.1.call-start
  39.2 4.6 %fusion.16 = f32[64,64,64]{2,0,1:T(8,128)S(1)} fusion(f32[64,64,64]{2,1,0:T(8,128)} %reshape.238, f32[3,64,64]{2,1,0:T(8,128)S(1)} %copy-done.6), kind=kOutput, calls=%fused_computation.36 | convolution fusion | flops 201326592 | bytes 2129920 | tf_op jit(solution)/shard_map/ai,...ijk->...ajk/dot_general | solution.py:37
  43.7 5.6 %fusion.14 = f32[64,64,64]{2,1,0:T(8,128)} fusion(f32[64,64,64]{2,0,1:T(8,128)S(1)} %fusion.16, f32[3,64,64]{2,1,0:T(8,128)S(1)} %copy-done.6), kind=kOutput, calls=%fused_computation.34 | convolution fusion | flops 201326592 | bytes 3178496 | tf_op jit(solution)/shard_map/bj,...ajk->...abk/dot_general | solution.py:38
  49.3 3.3 reshape.239
  52.6 5.8 %fusion.21 = f32[64,64,64]{2,1,0:T(8,128)S(1)} fusion(f32[64,64,64]{2,1,0:T(8,128)} %reshape.239, f32[64,64,64]{2,1,0:T(8,128)} %fusion.14, f32[3,64,64]{2,1,0:T(8,128)S(1)} %copy-done.6), kind=kOutput, calls=%fused_computation.42 | convolution fusion | flops 201588736 | bytes 3178496 | tf_op jit(solution)/shard_map/ck,...abk->...abc/dot_general | solution.py:39
  58.4 5.6 %fusion.18 = f32[64,64,64]{0,2,1:T(8,128)} fusion(f32[64,64,64]{2,1,0:T(8,128)S(1)} %fusion.21, f32[3,64,64]{2,1,0:T(8,128)S(1)} %copy-done.6), kind=kOutput, calls=%fused_computation.41 | convolution fusion | flops 201326592 | bytes 3178496 | tf_op jit(solution)/shard_map/ai,...ajk->...ijk/dot_general | solution.py:43
  64.0 4.3 %copy.80 = f32[64,64,64]{1,2,0:T(8,128)} copy(f32[64,64,64]{0,2,1:T(8,128)} %fusion.18) | data formatting | bytes 2097152 | tf_op jit(solution)/shard_map/ai,...ajk->...ijk/dot_general | solution.py:43
  68.4 4.7 %fusion.40 = f32[64,64,64]{2,1,0:T(8,128)} fusion(f32[64,64,64]{1,2,0:T(8,128)} %copy.80, f32[3,64,64]{2,1,0:T(8,128)S(1)} %copy-done.6), kind=kOutput, calls=%fused_computation.73 | convolution fusion | flops 201326592 | bytes 2129920 | tf_op jit(solution)/shard_map/bj,...ibk->...ijk/dot_general | solution.py:44
  73.1 88.8 %all-reduce.6.cloned.1.call-done = f32[192,128]{1,0:T(8,128)} async-done(((f32[192,128]{1,0:T(8,128)}), f32[192,128]{1,0:T(8,128)}) %all-reduce.6.cloned.1.call-update) | async-done | bytes 98320 | tf_op jit(solution)/shard_map/psum | solution.py:95
  161.9 1.5 gather_fusion
  163.4 2.7 fusion.62
  166.1 1.6 fusion.54
  167.7 1.4 scatter_custom_fusion.1
  169.1 3.5 fusion.8
  172.7 48.9 %all-reduce.8.cloned.1.call-done = f32[24576]{0:T(1024)} async-done(((f32[24576]{0:T(1024)}), f32[24576]{0:T(1024)}) %all-reduce.8.cloned.1.call-update) | async-done | bytes 98320 | tf_op jit(solution)/shard_map/psum | solution.py:96
  221.6 37.5 %all-reduce.10.cloned.1.call-done = f32[24576]{0:T(1024)} async-done(((f32[24576]{0:T(1024)}), f32[24576]{0:T(1024)}) %all-reduce.10.cloned.1.call-update) | async-done | bytes 98320 | tf_op jit(solution)/shard_map/psum | solution.py:96
  259.1 5.0 %gather_fusion.1 = f32[768]{0:T(1024)S(1)} fusion(f32[24576]{0:T(1024)} %all-reduce.10.cloned.1.call-done, s32[1024]{0:T(1024)S(1)} %pad_clamp_fusion), kind=kCustom, calls=%fused_computation.1 | custom fusion | bytes 9216 | tf_op jit(solution)/shard_map/gather | solution.py:97
  264.1 0.7 convolution_bitcast_fusion
  265.1 0.7 copy.126
  265.8 2.1 copy.95
  267.8 5.1 %scatter-add.48 = f32[64,64,64]{1,2,0:T(8,128)S(1)} dynamic-update-slice(f32[64,64,64]{1,2,0:T(8,128)S(1)} %constant_dynamic-update-slice_fusion.2, f32[64,1,64]{1,2,0:T(8,128)} %copy.95, s32[]{:T(128)} %constant.168.clone.1, s32[]{:T(128)} %constant.168.clone.1, s32[]{:T(128)} %constant.168.clone.1) | dynamic-update-slice | bytes 32772 | tf_op jit(solution)/shard_map/scatter-add | solution.py:76
  272.9 2.0 slice.283
  274.9 2.3 copy.127
  277.1 2.1 copy.97
  279.2 8.4 %scatter-add.49 = f32[64,64,64]{1,2,0:T(8,128)S(1)} dynamic-update-slice(f32[64,64,64]{1,2,0:T(8,128)S(1)} %scatter-add.48, f32[64,1,64]{1,2,0:T(8,128)} %copy.97, s32[]{:T(128)} %constant.168.clone.1, s32[]{:T(128)} %constant.171.clone.1, s32[]{:T(128)} %constant.168.clone.1) | dynamic-update-slice | bytes 32772 | tf_op jit(solution)/shard_map/scatter-add | solution.py:77
  288.1 3.3 collective-permute-start.1
  291.3 1.3 collective-permute-start
  292.9 4.2 %collective-permute-done = f32[1,64,64]{1,2,0:T(8,128)S(1)} collective-permute-done((f32[1,64,64]{1,2,0:T(8,128)S(1)}, f32[1,64,64]{1,2,0:T(8,128)S(1)}, u32[]{:S(2)}, u32[]{:S(2)}) %collective-permute-start) | collective-permute-done | bytes 16416 | tf_op jit(solution)/shard_map/ppermute | solution.py:21
  297.3 2.8 fusion.57
  300.1 2.8 copy.104
  302.9 2.8 copy.102
  305.7 1.3 collective-permute-start.2
  307.0 3.0 collective-permute-start.3
  310.0 1.3 broadcast_add_fusion
  311.3 3.1 copy.100
  314.4 2.2 add.101
  316.6 2.9 copy.101
  319.5 3.0 copy.105
  322.6 3.1 copy.103
  325.6 3.7 select_maximum_fusion
  329.4 0.4 copy-done.4
  329.8 0.6 copy-done.5
  330.4 6.5 %multiply_reduce_fusion = (f32[]{:T(128)}, f32[]{:T(128)}, f32[64,64,64]{1,2,0:T(8,128)}) fusion(f32[64,64,64]{1,2,0:T(8,128)S(1)} %scatter-add.51, f32[64,64,64]{1,2,0:T(8,128)S(1)} %copy-done.4, f32[66,66,66]{1,2,0:T(8,128)S(1)} %select_maximum_fusion, f32[1,64,64]{1,2,0:T(8,128)S(1)} %collective-permute-done, f32[1,64,64]{1,2,0:T(8,128)S(1)} %collective-permute-done.1, ...), kind=kLoop, calls=%fused_computation.39 | loop fusion | flops 5505022 | bytes 6358024 | tf_op jit(solution)/shard_map/reduce_sum | solution.py:112
  337.0 40.2 %all-reduce.1 = (f32[]{:T(128)}, f32[]{:T(128)}) all-reduce(f32[]{:T(128)} %get-tuple-element.75, f32[]{:T(128)} %get-tuple-element.74), channel_id=1, replica_groups=mesh['sub'=4,'cgrp'=8] {'sub','cgrp'}, use_global_device_ids=true, to_apply=%region_7.0 | all-reduce | flops 2 | bytes 16 | tf_op jit(solution)/shard_map/psum | solution.py:108
  378.5 5.4 %multiply_subtract_fusion = (f32[64,64,64]{1,2,0:T(8,128)}, f32[64,64,64]{1,2,0:T(8,128)}) fusion(f32[64,64,64]{1,2,0:T(8,128)} %copy.100, f32[64,64,64]{1,2,0:T(8,128)} %get-tuple-element.80, f32[]{:T(128)S(6)} %div.3, f32[64,64,64]{1,2,0:T(8,128)S(1)} %scatter-add.51), kind=kLoop, calls=%fused_computation.38 | loop fusion | flops 786432 | bytes 5242884 | tf_op jit(solution)/shard_map/sub | solution.py:129
  383.8 1.9 copy.110
  385.7 1.6 reshape.249
  387.4 3.1 copy.108
  390.5 2.9 reshape.248
  (57 shorter events, 2.1 us)
Async XLA Ops:
  7.2 156.2 %copy-start = (f32[6,8,128,128]{3,2,1,0:T(8,128)S(1)}, f32[6,8,128,128]{3,2,1,0:T(8,128)}, u32[]{:S(2)}) copy-start(f32[6,8,128,128]{3,2,1,0:T(8,128)} %param.27) | copy-start | bytes 9437188
  7.2 154.7 %all-reduce.6.cloned.1.call-start = ((), (), s32[]{:S(2)}) async-start(), calls=%async_computation | async-start | bytes 196608 | tf_op jit(solution)/shard_map/psum | solution.py:95
  13.2 5.0 %copy-start.9 = (s32[1,1,6,128]{3,1,2,0:T(1,128)S(1)}, s32[1,1,6,128]{3,1,2,0:T(1,128)}, u32[]{:S(2)}) copy-start(s32[1,1,6,128]{3,1,2,0:T(1,128)} %param.25) | copy-start | bytes 9220
  13.2 5.0 %copy-start.7 = (f32[2,128,64]{1,2,0:T(8,128)S(1)}, f32[2,128,64]{1,2,0:T(8,128)}, u32[]{:S(2)}) copy-start(f32[2,128,64]{1,2,0:T(8,128)} %param.24) | copy-start | bytes 196612
  21.3 17.7 %copy-start.8 = (s32[6,8]{1,0:T(8,128)S(1)}, s32[6,8]{1,0:T(8,128)}, u32[]{:S(2)}) copy-start(s32[6,8]{1,0:T(8,128)} %param.26) | copy-start | bytes 580
  21.3 17.8 %copy-start.6 = (f32[3,64,64]{2,1,0:T(8,128)S(1)}, f32[3,64,64]{2,1,0:T(8,128)}, u32[]{:S(2)}) copy-start(f32[3,64,64]{2,1,0:T(8,128)} %param.23) | copy-start | bytes 147460
  38.5 183.1 %all-reduce.8.cloned.1.call-start = ((), (), s32[]{:S(2)}) async-start(), calls=%async_computation.1 | async-start | bytes 196608 | tf_op jit(solution)/shard_map/psum | solution.py:96
  169.0 90.0 %all-reduce.10.cloned.1.call-start = ((), (), s32[]{:S(2)}) async-start(), calls=%async_computation.2 | async-start | bytes 196608 | tf_op jit(solution)/shard_map/psum | solution.py:96
  288.1 4.9 %collective-permute-start.1 = (f32[1,64,64]{1,2,0:T(8,128)S(1)}, f32[1,64,64]{1,2,0:T(8,128)S(1)}, u32[]{:S(2)}, u32[]{:S(2)}) collective-permute-start(f32[1,64,64]{1,2,0:T(8,128)S(1)} %get-tuple-element.83), channel_id=1, source_target_pairs={{0,8},{8,16},{16,24},{1,9},{9,17},{17,25},{2,10},{10,18},{18,26},{... | collective-permute-start | bytes 49160 | tf_op jit(solution)/shard_map/ppermute | solution.py:20
  291.3 5.8 %collective-permute-start = (f32[1,64,64]{1,2,0:T(8,128)S(1)}, f32[1,64,64]{1,2,0:T(8,128)S(1)}, u32[]{:S(2)}, u32[]{:S(2)}) collective-permute-start(f32[1,64,64]{1,2,0:T(8,128)S(1)} %get-tuple-element.84), channel_id=1, source_target_pairs={{8,0},{16,8},{24,16},{9,1},{17,9},{25,17},{10,2},{18,10},{26,18},{... | collective-permute-start | bytes 49160 | tf_op jit(solution)/shard_map/ppermute | solution.py:21
  305.7 16.9 %collective-permute-start.2 = (f32[66,1,64]{0,2,1:T(8,128)S(1)}, f32[66,1,64]{0,2,1:T(8,128)S(1)}, u32[]{:S(2)}, u32[]{:S(2)}) collective-permute-start(f32[66,1,64]{0,2,1:T(8,128)S(1)} %copy.102), channel_id=1, source_target_pairs={{1,0},{2,1},{3,2},{4,3},{5,4},{6,5},{7,6},{9,8},{10,9},{11,10},{12... | collective-permute-start | bytes 50696 | tf_op jit(solution)/shard_map/ppermute | solution.py:21
  307.0 12.6 %collective-permute-start.3 = (f32[66,1,64]{0,2,1:T(8,128)S(1)}, f32[66,1,64]{0,2,1:T(8,128)S(1)}, u32[]{:S(2)}, u32[]{:S(2)}) collective-permute-start(f32[66,1,64]{0,2,1:T(8,128)S(1)} %copy.104), channel_id=1, source_target_pairs={{0,1},{1,2},{2,3},{3,4},{4,5},{5,6},{6,7},{8,9},{9,10},{10,11},{11... | collective-permute-start | bytes 50696 | tf_op jit(solution)/shard_map/ppermute | solution.py:20
  325.6 3.8 copy-start.2
  325.6 3.8 copy-start.3
  325.6 4.2 %copy-start.4 = (f32[64,64,64]{1,2,0:T(8,128)S(1)}, f32[64,64,64]{1,2,0:T(8,128)}, u32[]{:S(2)}) copy-start(f32[64,64,64]{1,2,0:T(8,128)} %copy.100) | copy-start | bytes 3145732
  325.6 4.8 %copy-start.5 = (f32[64,64,64]{1,2,0:T(8,128)S(1)}, f32[64,64,64]{1,2,0:T(8,128)}, u32[]{:S(2)}) copy-start(f32[64,64,64]{1,2,0:T(8,128)} %copy.101) | copy-start | bytes 3145732
  387.4 6.0 %copy-start.1 = (f32[6,8,128,128]{3,2,1,0:T(8,128)S(1)}, f32[6,8,128,128]{3,2,1,0:T(8,128)}, u32[]{:S(2)}) copy-start(f32[6,8,128,128]{3,2,1,0:T(8,128)} %param.27) | copy-start | bytes 9437188
Sparse Core Ops, SparseCore 0:
  38.6 123.2 all-reduce.5
  169.2 52.3 all-reduce.7
  224.0 35.0 all-reduce.9
